TPU v7x, 128 devices: a whole 4x4x4 slice. The times are simulated.
128 devices in a mesh: row: 8 (over x_lo, z), col: 8 (over y, x_hi), depth: 2 (over core).
Axes of the slice: x: 4 (x_hi: 2, x_lo: 2; x = x_hi * 2 + x_lo), y: 4, z: 4, core: 2. Of those that a mesh axis runs over, the one named last changes fastest.
Arguments:
- tokens: bfloat16 [2048, 12288], P('col', ('row', 'depth')), may hold values from -6 to 6
- up_weight: bfloat16 [12288, 24576], P(('row', 'depth'), 'col'), may hold values from -0.0546875 to 0.0546875
- up_bias: float32 [24576], P('col'), may hold values from -3 to 3
- down_weight: bfloat16 [24576, 12288], P('col', ('row', 'depth')), may hold values from -0.0390625 to 0.0390625
- down_bias: float32 [12288], P(('row', 'depth')), may hold values from -3 to 3
Outputs:
- block_output: float32 [2048, 12288], P('col', ('row', 'depth'))
All inputs are finite; a program needn't handle non-finite values.
Results may differ from a plain program's by a relative error of at most 0.0025.
Values may be sent and summed in bfloat16 or wider, within the bound.
No kernel may reach another device: no remote copies, remote signals or barrier semaphores. Data moves between devices by JAX's collectives and lax.ppermute only.
A program may use at most 128 MiB of HBM per device.

v0:
```python
import jax
import jax.numpy as jnp
from jax import lax
from jax.experimental import pallas as pl
from jax.experimental.pallas import tpu as pltpu
from jax.sharding import PartitionSpec as P

BF, F16, F32 = jnp.bfloat16, jnp.float16, jnp.float32
SCALE = 16.0

ROW = {
    "x": [(i, i ^ 8) for i in range(16)],
    "p": [(i, i ^ (6 if i & 1 else 2)) for i in range(16)],
    "q": [(i, i ^ (2 if i & 1 else 6)) for i in range(16)],
}
COL = {
    "x": [(i, i ^ 2) for i in range(16)],
    "p": [(i, i ^ (12 if i & 1 else 4)) for i in range(16)],
    "q": [(i, i ^ (4 if i & 1 else 12)) for i in range(16)],
}
SWAP = [(0, 1), (1, 0)]

UNITS = (2, 2, 2, 2)
LAYOUTS = ("pxq", "pxq", "pxq", "pxq")
TOKEN_ORDER, OUT_ORDER = "xpq", "pqx"
ORDER = tuple(map(int, "0142031202140313021320312013201203243103201310231231230"))


def row_swap(v, d):
    return lax.ppermute(v, ("row", "depth"), ROW[d])


def col_swap(v, d):
    return lax.ppermute(v, ("col", "depth"), COL[d])


def up_kernel(x, own, other, keep, send):
    k, rows = own.shape[0], keep.shape[0]
    acc = jnp.dot(x[:, :k], own[...], preferred_element_type=F32)
    acc = acc + jnp.dot(x[:, k:], other[...], preferred_element_type=F32)
    acc = SCALE * acc
    keep[...] = acc[:rows]
    send[...] = acc[rows:]


def up_project(x, own, other):
    (m, k2), n, block = x.shape, own.shape[1], 1024
    half = jax.ShapeDtypeStruct((m // 2, n), F32)
    weight = pl.BlockSpec((k2 // 2, block), lambda i: (0, i))
    out = pl.BlockSpec((m // 2, block), lambda i: (0, i))
    return pl.pallas_call(
        up_kernel,
        grid=(n // block,),
        in_specs=[pl.BlockSpec((m, k2), lambda i: (0, 0)), weight, weight],
        out_specs=[out, out],
        out_shape=[half, half],
        compiler_params=pltpu.CompilerParams(vmem_limit_bytes=32 << 20),
    )(x, own, other)


class Chain:
    def __init__(self, token):
        self.token = token

    def after(self, *values):
        *values, self.token = lax.optimization_barrier((*values, self.token))
        return values[0] if len(values) == 1 else values


def chunk(chain, piece, up, up_bias, down, flip, layout, results):
    u, k = piece.shape
    held, dims = chain.after(piece), ""
    for d in TOKEN_ORDER:
        other = col_swap(chain.after(held), d)
        yield
        held, other = chain.after(held, other)
        new = "".join(c for c in layout if c in dims + d)
        at = new.index(d)
        shape = (2**at, held.shape[0] // 2**at, k)
        mine, theirs = held.reshape(shape), other.reshape(shape)
        low = jnp.where(flip[d], theirs, mine)
        high = jnp.where(flip[d], mine, theirs)
        held = chain.after(jnp.stack([low, high], 1).reshape(-1, k))
        dims = new
    held, send = up_project(held, *up)
    for d in layout:
        if d != layout[0]:
            rows = held.shape[0] // 2
            send, held = held[rows:], held[:rows]
        send, held = chain.after(send.astype(F16), held)
        got = row_swap(send, d)
        yield
        held, got = chain.after(held, got)
        held = held + got.astype(F32)
    held = jax.nn.gelu(held * (1 / SCALE) + up_bias, approximate=True).astype(BF)
    for d in reversed(layout):
        other = row_swap(chain.after(held), d)
        yield
        held, other = chain.after(held, other)
        held = chain.after(jnp.concatenate([held, other], 0))
    held, dims = jnp.stack([jnp.dot(held, w, preferred_element_type=F32) for w in down]), layout
    for d in OUT_ORDER:
        at, (_, rows, n) = dims.index(d), held.shape
        parts = held.reshape(2, 2**at, 2, rows // 2 ** (at + 1), n)
        low, high = parts[:, :, 0], parts[:, :, 1]
        send = jnp.where(flip[d], low, high).astype(BF).reshape(2, rows // 2, n)
        held = jnp.where(flip[d], high, low).reshape(2, rows // 2, n)
        send, held = chain.after(send, held)
        got = col_swap(send, d)
        yield
        held, got = chain.after(held, got)
        held = held + got.astype(F32)
        dims = dims.replace(d, "")
    results.append(chain.after(held))


def fetch(chain, up, down):
    for w in (up, down):
        other = lax.ppermute(chain.after(w[0]), "depth", SWAP)
        yield
        w.append(chain.after(jnp.where(chain.token, chain.after(other), jnp.zeros_like(other))))


def body(tokens, up_weight, up_bias, down_weight, down_bias):
    row, col, depth = (lax.axis_index(a) for a in ("row", "col", "depth"))
    zy = (row % 4) ^ (col // 2)
    b_bit = zy // 2
    a_bit = (zy % 2) ^ b_bit
    flip = {
        "x": ((row // 4) ^ (col % 2)) == 1,
        "p": jnp.where(depth == 0, a_bit, b_bit) == 1,
        "q": jnp.where(depth == 0, b_bit, a_bit) == 1,
    }
    half = tokens.shape[0] // 2

    give = lax.dynamic_slice_in_dim(tokens, (1 - depth) * half, half, 0)
    keep = lax.dynamic_slice_in_dim(tokens, depth * half, half, 0)
    mine = jnp.concatenate([keep, lax.ppermute(give, "depth", SWAP)], 1)
    chain = Chain(row < 8)
    up, down = [up_weight], [down_weight]
    weights = fetch(chain, up, down)

    results, steps, at = [[] for _ in UNITS], [], 0
    for units, layout, result in zip(UNITS, LAYOUTS, results):
        piece = mine[at : at + 16 * units]
        steps.append(chunk(chain, piece, up, up_bias, down, flip, layout, result))
        at += 16 * units
    steps.append(weights)
    for i in ORDER:
        next(steps[i], None)
    out = jnp.concatenate([r[0] for r in results], 1)
    own, other = out[0], out[1]
    got = lax.ppermute(other, "depth", SWAP)
    first = jnp.where(depth == 0, own, got)
    last = jnp.where(depth == 0, got, own)
    return jnp.where(chain.token, jnp.concatenate([first, last], 0) + down_bias, 0.0)


def solution(mesh):
    placed = (
        P("col", ("row", "depth")),
        P(("row", "depth"), "col"),
        P("col"),
        P("col", ("row", "depth")),
        P(("row", "depth")),
    )
    return jax.shard_map(
        body, mesh=mesh, in_specs=placed, out_specs=P("col", ("row", "depth")), check_vma=False
    )
```

profile of v0, /device:TPU:1, one launch (start us, length us, event | category | flops | bytes accessed | tf_op | source)
XLA Modules:
  0.0 178.1 jit_solution(17645589493832817664)
XLA Ops:
  4.1 2.8 %collective-permute-start.1 = (bf16[32,1536]{1,0:T(8,128)(2,1)S(1)}, bf16[32,1536]{1,0:T(8,128)(2,1)S(1)}, u32[]{:S(2)}, u32[]{:S(2)}) collective-permute-start(bf16[32,1536]{1,0:T(8,128)(2,1)S(1)} %get-tuple-element.340), channel_id=1, source_target_pairs={{0,2},{1,3},{2,0},{3,1},{4,6},{5,7},{6,4},{7,5},{8,10},{9,11},{10,... | collective-permute-start | bytes 294920 | tf_op jit(solution)/shard_map/ppermute | solution.py:34
  7.1 2.8 %collective-permute-start.4 = (bf16[32,1536]{1,0:T(8,128)(2,1)S(1)}, bf16[32,1536]{1,0:T(8,128)(2,1)S(1)}, u32[]{:S(2)}, u32[]{:S(2)}) collective-permute-start(bf16[32,1536]{1,0:T(8,128)(2,1)S(1)} %get-tuple-element.351), channel_id=1, source_target_pairs={{0,2},{1,3},{2,0},{3,1},{4,6},{5,7},{6,4},{7,5},{8,10},{9,11},{10,... | collective-permute-start | bytes 294920 | tf_op jit(solution)/shard_map/ppermute | solution.py:34
  10.0 2.9 %collective-permute-start.2 = (bf16[64,1536]{1,0:T(8,128)(2,1)S(1)}, bf16[64,1536]{1,0:T(8,128)(2,1)S(1)}, u32[]{:S(2)}, u32[]{:S(2)}) collective-permute-start(bf16[64,1536]{1,0:T(8,128)(2,1)S(1)} %bitcast.328), channel_id=1, source_target_pairs={{0,4},{1,13},{2,6},{3,15},{4,0},{5,9},{6,2},{7,11},{8,12},{9,5},{1... | collective-permute-start | bytes 589832 | tf_op jit(solution)/shard_map/ppermute | solution.py:34
  14.6 2.8 %collective-permute-start.6 = (bf16[64,1536]{1,0:T(8,128)(2,1)S(1)}, bf16[64,1536]{1,0:T(8,128)(2,1)S(1)}, u32[]{:S(2)}, u32[]{:S(2)}) collective-permute-start(bf16[64,1536]{1,0:T(8,128)(2,1)S(1)} %bitcast.326), channel_id=1, source_target_pairs={{0,4},{1,13},{2,6},{3,15},{4,0},{5,9},{6,2},{7,11},{8,12},{9,5},{1... | collective-permute-start | bytes 589832 | tf_op jit(solution)/shard_map/ppermute | solution.py:34
  20.1 3.3 %collective-permute-done.7 = bf16[64,1536]{1,0:T(8,128)(2,1)S(1)} collective-permute-done((bf16[64,1536]{1,0:T(8,128)(2,1)S(1)}, bf16[64,1536]{1,0:T(8,128)(2,1)S(1)}, u32[]{:S(2)}, u32[]{:S(2)}) %collective-permute-start.7) | collective-permute-done | bytes 196640 | tf_op jit(solution)/shard_map/ppermute | solution.py:34
  25.2 2.6 %broadcast_select_fusion.1.other = bf16[768,3072]{1,0:T(8,128)(2,1)S(1)} fusion(bf16[768,3072]{1,0:T(8,128)(2,1)} %collective-permute-done.8, pred[]{:T(512)S(6)} %lt.28), kind=kLoop, calls=%fused_computation.1 | loop fusion | flops 2359296 | bytes 9437185 | tf_op jit(solution)/shard_map/jit(_where)/select_n | solution.py:121
  28.0 3.8 %shard_map.55 = (f32[128,3072]{1,0:T(8,128)S(1)}, f32[128,3072]{1,0:T(8,128)S(1)}) custom-call(bf16[256,1536]{1,0:T(8,128)(2,1)S(1)} %bitcast.271, bf16[768,3072]{1,0:T(8,128)(2,1)S(1)} %bitcast.269, bf16[768,3072]{1,0:T(8,128)(2,1)S(1)} %broadcast_select_fusion.1.other), custom_call_target="tpu_custom_call" | custom-call | tf_op jit(solution)/shard_map/pallas_call | solution.py:51
  31.9 3.8 %collective-permute-start.9 = (f16[128,3072]{1,0:T(8,128)(2,1)S(1)}, f16[128,3072]{1,0:T(8,128)(2,1)S(1)}, u32[]{:S(2)}, u32[]{:S(2)}) collective-permute-start(f16[128,3072]{1,0:T(8,128)(2,1)S(1)} %convert_element_type.204), channel_id=1, source_target_pairs={{0,16},{1,49},{16,0},{17,33},{32,48},{33,17},{48,32},{49,1},{64,80... | collective-permute-start | bytes 2359304 | tf_op jit(solution)/shard_map/ppermute | solution.py:30
  35.8 2.5 %collective-permute-start.11 = (bf16[64,1536]{1,0:T(8,128)(2,1)S(1)}, bf16[64,1536]{1,0:T(8,128)(2,1)S(1)}, u32[]{:S(2)}, u32[]{:S(2)}) collective-permute-start(bf16[64,1536]{1,0:T(8,128)(2,1)S(1)} %bitcast.330), channel_id=1, source_target_pairs={{0,4},{1,13},{2,6},{3,15},{4,0},{5,9},{6,2},{7,11},{8,12},{9,5},{1... | collective-permute-start | bytes 589832 | tf_op jit(solution)/shard_map/ppermute | solution.py:34
  38.5 3.8 %shard_map.56 = (f32[128,3072]{1,0:T(8,128)S(1)}, f32[128,3072]{1,0:T(8,128)S(1)}) custom-call(bf16[256,1536]{1,0:T(8,128)(2,1)S(1)} %bitcast.272, bf16[768,3072]{1,0:T(8,128)(2,1)S(1)} %bitcast.269, bf16[768,3072]{1,0:T(8,128)(2,1)S(1)} %broadcast_select_fusion.1.other), custom_call_target="tpu_custom_call" | custom-call | tf_op jit(solution)/shard_map/pallas_call | solution.py:51
  46.4 3.8 %shard_map.57 = (f32[128,3072]{1,0:T(8,128)S(1)}, f32[128,3072]{1,0:T(8,128)S(1)}) custom-call(bf16[256,1536]{1,0:T(8,128)(2,1)S(1)} %bitcast.273, bf16[768,3072]{1,0:T(8,128)(2,1)S(1)} %bitcast.269, bf16[768,3072]{1,0:T(8,128)(2,1)S(1)} %broadcast_select_fusion.1.other), custom_call_target="tpu_custom_call" | custom-call | tf_op jit(solution)/shard_map/pallas_call | solution.py:51
  50.3 2.7 %collective-permute-start.15 = (f16[128,3072]{1,0:T(8,128)(2,1)S(1)}, f16[128,3072]{1,0:T(8,128)(2,1)S(1)}, u32[]{:S(2)}, u32[]{:S(2)}) collective-permute-start(f16[128,3072]{1,0:T(8,128)(2,1)S(1)} %convert_element_type.207), channel_id=1, source_target_pairs={{0,16},{1,49},{16,0},{17,33},{32,48},{33,17},{48,32},{49,1},{64,80... | collective-permute-start | bytes 2359304 | tf_op jit(solution)/shard_map/ppermute | solution.py:30
  55.0 3.8 %shard_map.58 = (f32[128,3072]{1,0:T(8,128)S(1)}, f32[128,3072]{1,0:T(8,128)S(1)}) custom-call(bf16[256,1536]{1,0:T(8,128)(2,1)S(1)} %bitcast.270, bf16[768,3072]{1,0:T(8,128)(2,1)S(1)} %bitcast.269, bf16[768,3072]{1,0:T(8,128)(2,1)S(1)} %broadcast_select_fusion.1.other), custom_call_target="tpu_custom_call" | custom-call | tf_op jit(solution)/shard_map/pallas_call | solution.py:51
  64.2 9.3 %collective-permute-done.21 = f16[128,3072]{1,0:T(8,128)(2,1)S(1)} collective-permute-done((f16[128,3072]{1,0:T(8,128)(2,1)S(1)}, f16[128,3072]{1,0:T(8,128)(2,1)S(1)}, u32[]{:S(2)}, u32[]{:S(2)}) %collective-permute-start.21) | collective-permute-done | bytes 786464 | tf_op jit(solution)/shard_map/ppermute | solution.py:30
  80.3 5.0 %collective-permute-done.24 = f16[64,3072]{1,0:T(8,128)(2,1)S(1)} collective-permute-done((f16[64,3072]{1,0:T(8,128)(2,1)S(1)}, f16[64,3072]{1,0:T(8,128)(2,1)S(1)}, u32[]{:S(2)}, u32[]{:S(2)}) %collective-permute-start.24) | collective-permute-done | bytes 393248 | tf_op jit(solution)/shard_map/ppermute | solution.py:30
  91.3 3.2 %collective-permute-done.27 = bf16[32,3072]{1,0:T(8,128)(2,1)S(1)} collective-permute-done((bf16[32,3072]{1,0:T(8,128)(2,1)S(1)}, bf16[32,3072]{1,0:T(8,128)(2,1)S(1)}, u32[]{:S(2)}, u32[]{:S(2)}) %collective-permute-start.27) | collective-permute-done | bytes 196640 | tf_op jit(solution)/shard_map/ppermute | solution.py:30
  96.8 14.1 %collective-permute-done.33 = bf16[64,3072]{1,0:T(8,128)(2,1)S(1)} collective-permute-done((bf16[64,3072]{1,0:T(8,128)(2,1)S(1)}, bf16[64,3072]{1,0:T(8,128)(2,1)S(1)}, u32[]{:S(2)}, u32[]{:S(2)}) %collective-permute-start.33) | collective-permute-done | bytes 393248 | tf_op jit(solution)/shard_map/ppermute | solution.py:30
  120.4 2.7 %collective-permute-done.36 = bf16[128,3072]{1,0:T(8,128)(2,1)S(1)} collective-permute-done((bf16[128,3072]{1,0:T(8,128)(2,1)S(1)}, bf16[128,3072]{1,0:T(8,128)(2,1)S(1)}, u32[]{:S(2)}, u32[]{:S(2)}) %collective-permute-start.36) | collective-permute-done | bytes 786464 | tf_op jit(solution)/shard_map/ppermute | solution.py:30
  127.4 3.0 %collective-permute-start.44 = (bf16[2,128,768]{2,1,0:T(8,128)(2,1)S(1)}, bf16[2,128,768]{2,1,0:T(8,128)(2,1)S(1)}, u32[]{:S(2)}, u32[]{:S(2)}) collective-permute-start(bf16[2,128,768]{2,1,0:T(8,128)(2,1)S(1)} %fusion.38), channel_id=1, source_target_pairs={{0,4},{1,13},{2,6},{3,15},{4,0},{5,9},{6,2},{7,11},{8,12},{9,5},{1... | collective-permute-start | bytes 1179656 | tf_op jit(solution)/shard_map/ppermute | solution.py:34
  134.8 5.2 %collective-permute-done.41 = bf16[128,3072]{1,0:T(8,128)(2,1)S(1)} collective-permute-done((bf16[128,3072]{1,0:T(8,128)(2,1)S(1)}, bf16[128,3072]{1,0:T(8,128)(2,1)S(1)}, u32[]{:S(2)}, u32[]{:S(2)}) %collective-permute-start.41) | collective-permute-done | bytes 786464 | tf_op jit(solution)/shard_map/ppermute | solution.py:30
  147.0 5.9 %collective-permute-done.43 = bf16[2,128,768]{2,1,0:T(8,128)(2,1)S(1)} collective-permute-done((bf16[2,128,768]{2,1,0:T(8,128)(2,1)S(1)}, bf16[2,128,768]{2,1,0:T(8,128)(2,1)S(1)}, u32[]{:S(2)}, u32[]{:S(2)}) %collective-permute-start.43) | collective-permute-done | bytes 393248 | tf_op jit(solution)/shard_map/ppermute | solution.py:34
  156.5 3.6 %collective-permute-done.45 = bf16[2,64,768]{2,1,0:T(8,128)(2,1)S(1)} collective-permute-done((bf16[2,64,768]{2,1,0:T(8,128)(2,1)S(1)}, bf16[2,64,768]{2,1,0:T(8,128)(2,1)S(1)}, u32[]{:S(2)}, u32[]{:S(2)}) %collective-permute-start.45) | collective-permute-done | bytes 196640 | tf_op jit(solution)/shard_map/ppermute | solution.py:34
  161.5 3.7 %collective-permute-done.48 = bf16[2,32,768]{2,1,0:T(8,128)(2,1)S(1)} collective-permute-done((bf16[2,32,768]{2,1,0:T(8,128)(2,1)S(1)}, bf16[2,32,768]{2,1,0:T(8,128)(2,1)S(1)}, u32[]{:S(2)}, u32[]{:S(2)}) %collective-permute-start.48) | collective-permute-done | bytes 98336 | tf_op jit(solution)/shard_map/ppermute | solution.py:34
  165.4 10.3 %collective-permute-start.51 = (f32[128,768]{1,0:T(8,128)S(1)}, f32[128,768]{1,0:T(8,128)S(1)}, u32[]{:S(2)}, u32[]{:S(2)}) collective-permute-start(f32[128,768]{1,0:T(8,128)S(1)} %slice_bitcast_fusion), channel_id=1, source_target_pairs={{0,1},{1,0},{2,3},{3,2},{4,5},{5,4},{6,7},{7,6},{8,9},{9,8},{10,11... | collective-permute-start | bytes 1179656 | tf_op jit(solution)/shard_map/ppermute | solution.py:153
  (213 shorter events, 69.3 us)
Async XLA Ops:
  3.7 21.5 %collective-permute-start.8 = (bf16[768,3072]{1,0:T(8,128)(2,1)}, bf16[768,3072]{1,0:T(8,128)(2,1)}, u32[]{:S(2)}, u32[]{:S(2)}) collective-permute-start(bf16[768,3072]{1,0:T(8,128)(2,1)} %own.7), channel_id=1, source_target_pairs={{0,1},{1,0},{2,3},{3,2},{4,5},{5,4},{6,7},{7,6},{8,9},{9,8},{10,11... | collective-permute-start | bytes 14155784 | tf_op jit(solution)/shard_map/ppermute | solution.py:119
  17.5 18.3 %collective-permute-start.10 = (bf16[32,1536]{1,0:T(8,128)(2,1)S(1)}, bf16[32,1536]{1,0:T(8,128)(2,1)S(1)}, u32[]{:S(2)}, u32[]{:S(2)}) collective-permute-start(bf16[32,1536]{1,0:T(8,128)(2,1)S(1)} %get-tuple-element.395), channel_id=1, source_target_pairs={{0,2},{1,3},{2,0},{3,1},{4,6},{5,7},{6,4},{7,5},{8,10},{9,11},{10,... | collective-permute-start | bytes 294920 | tf_op jit(solution)/shard_map/ppermute | solution.py:34
  23.6 14.7 %collective-permute-start.12 = (bf16[128,1536]{1,0:T(8,128)(2,1)S(1)}, bf16[128,1536]{1,0:T(8,128)(2,1)S(1)}, u32[]{:S(2)}, u32[]{:S(2)}) collective-permute-start(bf16[128,1536]{1,0:T(8,128)(2,1)S(1)} %bitcast.310), channel_id=1, source_target_pairs={{0,12},{1,5},{2,14},{3,7},{4,8},{5,1},{6,10},{7,3},{8,4},{9,13},{1... | collective-permute-start | bytes 1179656 | tf_op jit(solution)/shard_map/ppermute | solution.py:34
  23.7 22.5 %collective-permute-start.14 = (bf16[128,1536]{1,0:T(8,128)(2,1)S(1)}, bf16[128,1536]{1,0:T(8,128)(2,1)S(1)}, u32[]{:S(2)}, u32[]{:S(2)}) collective-permute-start(bf16[128,1536]{1,0:T(8,128)(2,1)S(1)} %bitcast.306), channel_id=1, source_target_pairs={{0,12},{1,5},{2,14},{3,7},{4,8},{5,1},{6,10},{7,3},{8,4},{9,13},{1... | collective-permute-start | bytes 1179656 | tf_op jit(solution)/shard_map/ppermute | solution.py:34
  31.9 13.2 %collective-permute-start.9 = (f16[128,3072]{1,0:T(8,128)(2,1)S(1)}, f16[128,3072]{1,0:T(8,128)(2,1)S(1)}, u32[]{:S(2)}, u32[]{:S(2)}) collective-permute-start(f16[128,3072]{1,0:T(8,128)(2,1)S(1)} %convert_element_type.204), channel_id=1, source_target_pairs={{0,16},{1,49},{16,0},{17,33},{32,48},{33,17},{48,32},{49,1},{64,80... | collective-permute-start | bytes 2359304 | tf_op jit(solution)/shard_map/ppermute | solution.py:30
  42.4 12.1 %collective-permute-start.17 = (f16[128,3072]{1,0:T(8,128)(2,1)S(1)}, f16[128,3072]{1,0:T(8,128)(2,1)S(1)}, u32[]{:S(2)}, u32[]{:S(2)}) collective-permute-start(f16[128,3072]{1,0:T(8,128)(2,1)S(1)} %convert_element_type.205), channel_id=1, source_target_pairs={{0,16},{1,49},{16,0},{17,33},{32,48},{33,17},{48,32},{49,1},{64,80... | collective-permute-start | bytes 2359304 | tf_op jit(solution)/shard_map/ppermute | solution.py:30
  42.6 68.5 %collective-permute-start.34 = (bf16[3072,768]{1,0:T(8,128)(2,1)S(1)}, bf16[3072,768]{1,0:T(8,128)(2,1)S(1)}, u32[]{:S(2)}, u32[]{:S(2)}) collective-permute-start(bf16[3072,768]{1,0:T(8,128)(2,1)S(1)} %bitcast.339), channel_id=1, source_target_pairs={{0,1},{1,0},{2,3},{3,2},{4,5},{5,4},{6,7},{7,6},{8,9},{9,8},{10,11... | collective-permute-start | bytes 14155784 | tf_op jit(solution)/shard_map/ppermute | solution.py:119
  42.8 12.1 %collective-permute-start.16 = (bf16[128,1536]{1,0:T(8,128)(2,1)S(1)}, bf16[128,1536]{1,0:T(8,128)(2,1)S(1)}, u32[]{:S(2)}, u32[]{:S(2)}) collective-permute-start(bf16[128,1536]{1,0:T(8,128)(2,1)S(1)} %bitcast.308), channel_id=1, source_target_pairs={{0,12},{1,5},{2,14},{3,7},{4,8},{5,1},{6,10},{7,3},{8,4},{9,13},{1... | collective-permute-start | bytes 1179656 | tf_op jit(solution)/shard_map/ppermute | solution.py:34
  45.5 17.8 %collective-permute-start.13 = (f16[64,3072]{1,0:T(8,128)(2,1)S(1)}, f16[64,3072]{1,0:T(8,128)(2,1)S(1)}, u32[]{:S(2)}, u32[]{:S(2)}) collective-permute-start(f16[64,3072]{1,0:T(8,128)(2,1)S(1)} %get-tuple-element.418), channel_id=1, source_target_pairs={{0,64},{1,65},{16,80},{17,81},{32,96},{33,97},{48,112},{49,113},{6... | collective-permute-start | bytes 1179656 | tf_op jit(solution)/shard_map/ppermute | solution.py:30
  50.3 12.7 %collective-permute-start.15 = (f16[128,3072]{1,0:T(8,128)(2,1)S(1)}, f16[128,3072]{1,0:T(8,128)(2,1)S(1)}, u32[]{:S(2)}, u32[]{:S(2)}) collective-permute-start(f16[128,3072]{1,0:T(8,128)(2,1)S(1)} %convert_element_type.207), channel_id=1, source_target_pairs={{0,16},{1,49},{16,0},{17,33},{32,48},{33,17},{48,32},{49,1},{64,80... | collective-permute-start | bytes 2359304 | tf_op jit(solution)/shard_map/ppermute | solution.py:30
  58.9 14.9 %collective-permute-start.20 = (f16[64,3072]{1,0:T(8,128)(2,1)S(1)}, f16[64,3072]{1,0:T(8,128)(2,1)S(1)}, u32[]{:S(2)}, u32[]{:S(2)}) collective-permute-start(f16[64,3072]{1,0:T(8,128)(2,1)S(1)} %get-tuple-element.460), channel_id=1, source_target_pairs={{0,64},{1,65},{16,80},{17,81},{32,96},{33,97},{48,112},{49,113},{6... | collective-permute-start | bytes 1179656 | tf_op jit(solution)/shard_map/ppermute | solution.py:30
  59.6 13.9 %collective-permute-start.21 = (f16[128,3072]{1,0:T(8,128)(2,1)S(1)}, f16[128,3072]{1,0:T(8,128)(2,1)S(1)}, u32[]{:S(2)}, u32[]{:S(2)}) collective-permute-start(f16[128,3072]{1,0:T(8,128)(2,1)S(1)} %convert_element_type.209), channel_id=1, source_target_pairs={{0,16},{1,49},{16,0},{17,33},{32,48},{33,17},{48,32},{49,1},{64,80... | collective-permute-start | bytes 2359304 | tf_op jit(solution)/shard_map/ppermute | solution.py:30
  63.4 13.1 %collective-permute-start.18 = (f16[32,3072]{1,0:T(8,128)(2,1)S(1)}, f16[32,3072]{1,0:T(8,128)(2,1)S(1)}, u32[]{:S(2)}, u32[]{:S(2)}) collective-permute-start(f16[32,3072]{1,0:T(8,128)(2,1)S(1)} %get-tuple-element.456), channel_id=1, source_target_pairs={{0,48},{1,17},{16,32},{17,1},{32,16},{33,49},{48,0},{49,33},{64,11... | collective-permute-start | bytes 589832 | tf_op jit(solution)/shard_map/ppermute | solution.py:30
  63.5 12.8 %collective-permute-start.19 = (f16[64,3072]{1,0:T(8,128)(2,1)S(1)}, f16[64,3072]{1,0:T(8,128)(2,1)S(1)}, u32[]{:S(2)}, u32[]{:S(2)}) collective-permute-start(f16[64,3072]{1,0:T(8,128)(2,1)S(1)} %get-tuple-element.458), channel_id=1, source_target_pairs={{0,64},{1,65},{16,80},{17,81},{32,96},{33,97},{48,112},{49,113},{6... | collective-permute-start | bytes 1179656 | tf_op jit(solution)/shard_map/ppermute | solution.py:30
  90.4 21.0 %collective-permute-start.30 = (bf16[64,3072]{1,0:T(8,128)(2,1)S(1)}, bf16[64,3072]{1,0:T(8,128)(2,1)S(1)}, u32[]{:S(2)}, u32[]{:S(2)}) collective-permute-start(bf16[64,3072]{1,0:T(8,128)(2,1)S(1)} %pad_maximum_fusion.21), channel_id=1, source_target_pairs={{0,64},{1,65},{16,80},{17,81},{32,96},{33,97},{48,112},{49,113},{6... | collective-permute-start | bytes 1179656 | tf_op jit(solution)/shard_map/ppermute | solution.py:30
  94.6 16.3 %collective-permute-start.33 = (bf16[64,3072]{1,0:T(8,128)(2,1)S(1)}, bf16[64,3072]{1,0:T(8,128)(2,1)S(1)}, u32[]{:S(2)}, u32[]{:S(2)}) collective-permute-start(bf16[64,3072]{1,0:T(8,128)(2,1)S(1)} %pad_maximum_fusion.22), channel_id=1, source_target_pairs={{0,64},{1,65},{16,80},{17,81},{32,96},{33,97},{48,112},{49,113},{6... | collective-permute-start | bytes 1179656 | tf_op jit(solution)/shard_map/ppermute | solution.py:30
  95.9 15.6 %collective-permute-start.29 = (bf16[128,3072]{1,0:T(8,128)(2,1)S(1)}, bf16[128,3072]{1,0:T(8,128)(2,1)S(1)}, u32[]{:S(2)}, u32[]{:S(2)}) collective-permute-start(bf16[128,3072]{1,0:T(8,128)(2,1)S(1)} %pad_maximum_fusion.12), channel_id=1, source_target_pairs={{0,16},{1,49},{16,0},{17,33},{32,48},{33,17},{48,32},{49,1},{64,80... | collective-permute-start | bytes 2359304 | tf_op jit(solution)/shard_map/ppermute | solution.py:30
  96.7 14.7 %collective-permute-start.32 = (bf16[32,3072]{1,0:T(8,128)(2,1)S(1)}, bf16[32,3072]{1,0:T(8,128)(2,1)S(1)}, u32[]{:S(2)}, u32[]{:S(2)}) collective-permute-start(bf16[32,3072]{1,0:T(8,128)(2,1)S(1)} %fusion.37), channel_id=1, source_target_pairs={{0,48},{1,17},{16,32},{17,1},{32,16},{33,49},{48,0},{49,33},{64,11... | collective-permute-start | bytes 589832 | tf_op jit(solution)/shard_map/ppermute | solution.py:30
  110.9 12.1 %collective-permute-start.36 = (bf16[128,3072]{1,0:T(8,128)(2,1)S(1)}, bf16[128,3072]{1,0:T(8,128)(2,1)S(1)}, u32[]{:S(2)}, u32[]{:S(2)}) collective-permute-start(bf16[128,3072]{1,0:T(8,128)(2,1)S(1)} %pad_maximum_fusion.13), channel_id=1, source_target_pairs={{0,16},{1,49},{16,0},{17,33},{32,48},{33,17},{48,32},{49,1},{64,80... | collective-permute-start | bytes 2359304 | tf_op jit(solution)/shard_map/ppermute | solution.py:30
  117.3 14.2 %collective-permute-start.39 = (bf16[128,3072]{1,0:T(8,128)(2,1)S(1)}, bf16[128,3072]{1,0:T(8,128)(2,1)S(1)}, u32[]{:S(2)}, u32[]{:S(2)}) collective-permute-start(bf16[128,3072]{1,0:T(8,128)(2,1)S(1)} %pad_maximum_fusion.14), channel_id=1, source_target_pairs={{0,16},{1,49},{16,0},{17,33},{32,48},{33,17},{48,32},{49,1},{64,80... | collective-permute-start | bytes 2359304 | tf_op jit(solution)/shard_map/ppermute | solution.py:30
  126.4 16.9 %collective-permute-start.38 = (bf16[2,64,768]{2,1,0:T(8,128)(2,1)S(1)}, bf16[2,64,768]{2,1,0:T(8,128)(2,1)S(1)}, u32[]{:S(2)}, u32[]{:S(2)}) collective-permute-start(bf16[2,64,768]{2,1,0:T(8,128)(2,1)S(1)} %bitcast.334), channel_id=1, source_target_pairs={{0,12},{1,5},{2,14},{3,7},{4,8},{5,1},{6,10},{7,3},{8,4},{9,13},{1... | collective-permute-start | bytes 589832 | tf_op jit(solution)/shard_map/ppermute | solution.py:34
  126.5 13.4 %collective-permute-start.41 = (bf16[128,3072]{1,0:T(8,128)(2,1)S(1)}, bf16[128,3072]{1,0:T(8,128)(2,1)S(1)}, u32[]{:S(2)}, u32[]{:S(2)}) collective-permute-start(bf16[128,3072]{1,0:T(8,128)(2,1)S(1)} %pad_maximum_fusion.15), channel_id=1, source_target_pairs={{0,16},{1,49},{16,0},{17,33},{32,48},{33,17},{48,32},{49,1},{64,80... | collective-permute-start | bytes 2359304 | tf_op jit(solution)/shard_map/ppermute | solution.py:30
  127.4 17.9 %collective-permute-start.44 = (bf16[2,128,768]{2,1,0:T(8,128)(2,1)S(1)}, bf16[2,128,768]{2,1,0:T(8,128)(2,1)S(1)}, u32[]{:S(2)}, u32[]{:S(2)}) collective-permute-start(bf16[2,128,768]{2,1,0:T(8,128)(2,1)S(1)} %fusion.38), channel_id=1, source_target_pairs={{0,4},{1,13},{2,6},{3,15},{4,0},{5,9},{6,2},{7,11},{8,12},{9,5},{1... | collective-permute-start | bytes 1179656 | tf_op jit(solution)/shard_map/ppermute | solution.py:34
  143.4 21.8 %collective-permute-start.42 = (bf16[2,32,768]{2,1,0:T(8,128)(2,1)S(1)}, bf16[2,32,768]{2,1,0:T(8,128)(2,1)S(1)}, u32[]{:S(2)}, u32[]{:S(2)}) collective-permute-start(bf16[2,32,768]{2,1,0:T(8,128)(2,1)S(1)} %fusion.52), channel_id=1, source_target_pairs={{0,2},{1,3},{2,0},{3,1},{4,6},{5,7},{6,4},{7,5},{8,10},{9,11},{10,... | collective-permute-start | bytes 294920 | tf_op jit(solution)/shard_map/ppermute | solution.py:34
  (34 other events, 248.1 us)
where the time goes:
time: 178 us
  waiting for transfers between devices  71.8 us (40%)
  starting transfers between devices  67 us (38%)
  Pallas kernels  15.3 us (9%)
  matrix products  11.4 us (6%)
  other arithmetic  10.2 us (6%)
    ppermute x24, waiting for transfers between devices, row_swap(): return lax.ppermute(v, ('row', 'depth'), ROW[d])  51.2 us
    ppermute x24, starting transfers between devices, col_swap(): return lax.ppermute(v, ('col', 'depth'), COL[d])  30.4 us
    ppermute x24, starting transfers between devices, row_swap(): return lax.ppermute(v, ('row', 'depth'), ROW[d])  24.2 us
    ppermute x24, waiting for transfers between devices, col_swap(): return lax.ppermute(v, ('col', 'depth'), COL[d])  18.2 us
    pallas_call x4, Pallas kernels, up_project(): pl.pallas_call(up_kernel, grid=(n // block,), in_specs=[pl.BlockSpec((m,...  15.3 us
    dot_general x8, matrix products, chunk(): jnp.dot(held, w, preferred_element_type=F32)  11.4 us
    ppermute x1, starting transfers between devices, body(): got = lax.ppermute(other, 'depth', SWAP)  10.3 us
  transfers between devices with their start and end apart: 52, of which 21 were waited for; matrix products, arithmetic and copies ran while one was open for 12% of the time, Pallas kernels for 9%

commit v1 on v0

--- a/solution.py
+++ b/solution.py
@@ -118,7 +118,10 @@
     for w in (up, down):
         other = lax.ppermute(chain.after(w[0]), "depth", SWAP)
         yield
-        w.append(chain.after(jnp.where(chain.token, chain.after(other), jnp.zeros_like(other))))
+        other = chain.after(other)
+        if w is down:
+            other = chain.after(jnp.where(chain.token, other, jnp.zeros_like(other)))
+        w.append(other)
 
 
 def body(tokens, up_weight, up_bias, down_weight, down_bias):

time: 178 us -> 183 us (1.028)
  Pallas kernels: 15.3 us -> 20.7 us
  waiting for transfers between devices: 71.8 us -> 76.7 us
  starting transfers between devices: 67 us -> 63.9 us
  other arithmetic: 10.2 us -> 7.54 us
    pallas_call x4, Pallas kernels: 15.3 us -> 20.7 us  [up_project(): pl.pallas_call(up_kernel, grid=(n // block,), in_specs=[pl.BlockSpec((m,...]
    ppermute x24, waiting for transfers between devices: 18.2 us -> 20.9 us  [col_swap(): return lax.ppermute(v, ('col', 'depth'), COL[d])]
    select_n x2 -> x1, other arithmetic: 2.96 us -> 0.31 us  [fetch(): other = chain.after(jnp.where(chain.token, other, jnp.zeros_like(other)))]
    ppermute x24, waiting for transfers between devices: 51.2 us -> 53.4 us  [row_swap(): return lax.ppermute(v, ('row', 'depth'), ROW[d])]
    ppermute x1, starting transfers between devices: 10.3 us -> 8.46 us  [body(): got = lax.ppermute(other, 'depth', SWAP)]
  transfers between devices with their start and end apart: 52 -> 52, of which waited for: 21 -> 25; matrix products, arithmetic and copies ran while one was open for 12% -> 10% of each run, Pallas kernels for 9% -> 11%
where the time goes in v1:
time: 183 us
  waiting for transfers between devices  76.7 us (42%)
  starting transfers between devices  63.9 us (35%)
  Pallas kernels  20.7 us (11%)
  matrix products  11.4 us (6%)
  other arithmetic  7.54 us (4%)
    ppermute x24, waiting for transfers between devices, row_swap(): return lax.ppermute(v, ('row', 'depth'), ROW[d])  53.4 us
    ppermute x24, starting transfers between devices, col_swap(): return lax.ppermute(v, ('col', 'depth'), COL[d])  30.7 us
    ppermute x24, starting transfers between devices, row_swap(): return lax.ppermute(v, ('row', 'depth'), ROW[d])  22.7 us
    ppermute x24, waiting for transfers between devices, col_swap(): return lax.ppermute(v, ('col', 'depth'), COL[d])  20.9 us
    pallas_call x4, Pallas kernels, up_project(): pl.pallas_call(up_kernel, grid=(n // block,), in_specs=[pl.BlockSpec((m,...  20.7 us
    dot_general x8, matrix products, chunk(): jnp.dot(held, w, preferred_element_type=F32)  11.4 us
    ppermute x1, starting transfers between devices, body(): got = lax.ppermute(other, 'depth', SWAP)  8.46 us
  transfers between devices with their start and end apart: 52, of which 25 were waited for; matrix products, arithmetic and copies ran while one was open for 10% of the time, Pallas kernels for 11%

profile of v1, /device:TPU:1, one launch (start us, length us, event | category | flops | bytes accessed | tf_op | source)
XLA Modules:
  0.0 182.6 jit_solution(14739792679965807372)
XLA Ops:
  4.1 2.8 %collective-permute-start.1 = (bf16[32,1536]{1,0:T(8,128)(2,1)S(1)}, bf16[32,1536]{1,0:T(8,128)(2,1)S(1)}, u32[]{:S(2)}, u32[]{:S(2)}) collective-permute-start(bf16[32,1536]{1,0:T(8,128)(2,1)S(1)} %get-tuple-element.338), channel_id=1, source_target_pairs={{0,2},{1,3},{2,0},{3,1},{4,6},{5,7},{6,4},{7,5},{8,10},{9,11},{10,... | collective-permute-start | bytes 294920 | tf_op jit(solution)/shard_map/ppermute | solution.py:34
  7.1 2.8 %collective-permute-start.4 = (bf16[32,1536]{1,0:T(8,128)(2,1)S(1)}, bf16[32,1536]{1,0:T(8,128)(2,1)S(1)}, u32[]{:S(2)}, u32[]{:S(2)}) collective-permute-start(bf16[32,1536]{1,0:T(8,128)(2,1)S(1)} %get-tuple-element.349), channel_id=1, source_target_pairs={{0,2},{1,3},{2,0},{3,1},{4,6},{5,7},{6,4},{7,5},{8,10},{9,11},{10,... | collective-permute-start | bytes 294920 | tf_op jit(solution)/shard_map/ppermute | solution.py:34
  10.0 2.9 %collective-permute-start.2 = (bf16[64,1536]{1,0:T(8,128)(2,1)S(1)}, bf16[64,1536]{1,0:T(8,128)(2,1)S(1)}, u32[]{:S(2)}, u32[]{:S(2)}) collective-permute-start(bf16[64,1536]{1,0:T(8,128)(2,1)S(1)} %bitcast.326), channel_id=1, source_target_pairs={{0,4},{1,13},{2,6},{3,15},{4,0},{5,9},{6,2},{7,11},{8,12},{9,5},{1... | collective-permute-start | bytes 589832 | tf_op jit(solution)/shard_map/ppermute | solution.py:34
  14.6 2.8 %collective-permute-start.7 = (bf16[64,1536]{1,0:T(8,128)(2,1)S(1)}, bf16[64,1536]{1,0:T(8,128)(2,1)S(1)}, u32[]{:S(2)}, u32[]{:S(2)}) collective-permute-start(bf16[64,1536]{1,0:T(8,128)(2,1)S(1)} %bitcast.324), channel_id=1, source_target_pairs={{0,4},{1,13},{2,6},{3,15},{4,0},{5,9},{6,2},{7,11},{8,12},{9,5},{1... | collective-permute-start | bytes 589832 | tf_op jit(solution)/shard_map/ppermute | solution.py:34
  17.5 2.4 %collective-permute-start.10 = (bf16[32,1536]{1,0:T(8,128)(2,1)S(1)}, bf16[32,1536]{1,0:T(8,128)(2,1)S(1)}, u32[]{:S(2)}, u32[]{:S(2)}) collective-permute-start(bf16[32,1536]{1,0:T(8,128)(2,1)S(1)} %get-tuple-element.391), channel_id=1, source_target_pairs={{0,2},{1,3},{2,0},{3,1},{4,6},{5,7},{6,4},{7,5},{8,10},{9,11},{10,... | collective-permute-start | bytes 294920 | tf_op jit(solution)/shard_map/ppermute | solution.py:34
  20.1 3.3 %collective-permute-done.8 = bf16[64,1536]{1,0:T(8,128)(2,1)S(1)} collective-permute-done((bf16[64,1536]{1,0:T(8,128)(2,1)S(1)}, bf16[64,1536]{1,0:T(8,128)(2,1)S(1)}, u32[]{:S(2)}, u32[]{:S(2)}) %collective-permute-start.8) | collective-permute-done | bytes 196640 | tf_op jit(solution)/shard_map/ppermute | solution.py:34
  27.7 5.1 %shard_map.55 = (f32[128,3072]{1,0:T(8,128)S(1)}, f32[128,3072]{1,0:T(8,128)S(1)}) custom-call(bf16[256,1536]{1,0:T(8,128)(2,1)S(1)} %bitcast.269, bf16[768,3072]{1,0:T(8,128)(2,1)S(1)} %copy-done, bf16[768,3072]{1,0:T(8,128)(2,1)} %collective-permute-done.6.other), custom_call_target="tpu_custom_call" | custom-call | tf_op jit(solution)/shard_map/pallas_call | solution.py:51
  32.9 3.8 %collective-permute-start.9 = (f16[128,3072]{1,0:T(8,128)(2,1)S(1)}, f16[128,3072]{1,0:T(8,128)(2,1)S(1)}, u32[]{:S(2)}, u32[]{:S(2)}) collective-permute-start(f16[128,3072]{1,0:T(8,128)(2,1)S(1)} %convert_element_type.204), channel_id=1, source_target_pairs={{0,16},{1,49},{16,0},{17,33},{32,48},{33,17},{48,32},{49,1},{64,80... | collective-permute-start | bytes 2359304 | tf_op jit(solution)/shard_map/ppermute | solution.py:30
  36.8 2.8 %collective-permute-start.11 = (bf16[64,1536]{1,0:T(8,128)(2,1)S(1)}, bf16[64,1536]{1,0:T(8,128)(2,1)S(1)}, u32[]{:S(2)}, u32[]{:S(2)}) collective-permute-start(bf16[64,1536]{1,0:T(8,128)(2,1)S(1)} %bitcast.328), channel_id=1, source_target_pairs={{0,4},{1,13},{2,6},{3,15},{4,0},{5,9},{6,2},{7,11},{8,12},{9,5},{1... | collective-permute-start | bytes 589832 | tf_op jit(solution)/shard_map/ppermute | solution.py:34
  39.8 5.3 %shard_map.56 = (f32[128,3072]{1,0:T(8,128)S(1)}, f32[128,3072]{1,0:T(8,128)S(1)}) custom-call(bf16[256,1536]{1,0:T(8,128)(2,1)S(1)} %bitcast.270, bf16[768,3072]{1,0:T(8,128)(2,1)S(1)} %copy-done, bf16[768,3072]{1,0:T(8,128)(2,1)} %collective-permute-done.6.other), custom_call_target="tpu_custom_call" | custom-call | tf_op jit(solution)/shard_map/pallas_call | solution.py:51
  47.3 5.1 %shard_map.57 = (f32[128,3072]{1,0:T(8,128)S(1)}, f32[128,3072]{1,0:T(8,128)S(1)}) custom-call(bf16[256,1536]{1,0:T(8,128)(2,1)S(1)} %bitcast.271, bf16[768,3072]{1,0:T(8,128)(2,1)S(1)} %copy-done, bf16[768,3072]{1,0:T(8,128)(2,1)} %collective-permute-done.6.other), custom_call_target="tpu_custom_call" | custom-call | tf_op jit(solution)/shard_map/pallas_call | solution.py:51
  52.5 2.7 %collective-permute-start.15 = (f16[128,3072]{1,0:T(8,128)(2,1)S(1)}, f16[128,3072]{1,0:T(8,128)(2,1)S(1)}, u32[]{:S(2)}, u32[]{:S(2)}) collective-permute-start(f16[128,3072]{1,0:T(8,128)(2,1)S(1)} %convert_element_type.207), channel_id=1, source_target_pairs={{0,16},{1,49},{16,0},{17,33},{32,48},{33,17},{48,32},{49,1},{64,80... | collective-permute-start | bytes 2359304 | tf_op jit(solution)/shard_map/ppermute | solution.py:30
  57.8 5.1 %shard_map.58 = (f32[128,3072]{1,0:T(8,128)S(1)}, f32[128,3072]{1,0:T(8,128)S(1)}) custom-call(bf16[256,1536]{1,0:T(8,128)(2,1)S(1)} %bitcast.268, bf16[768,3072]{1,0:T(8,128)(2,1)S(1)} %copy-done, bf16[768,3072]{1,0:T(8,128)(2,1)} %collective-permute-done.6.other), custom_call_target="tpu_custom_call" | custom-call | tf_op jit(solution)/shard_map/pallas_call | solution.py:51
  67.2 10.7 %collective-permute-done.21 = f16[128,3072]{1,0:T(8,128)(2,1)S(1)} collective-permute-done((f16[128,3072]{1,0:T(8,128)(2,1)S(1)}, f16[128,3072]{1,0:T(8,128)(2,1)S(1)}, u32[]{:S(2)}, u32[]{:S(2)}) %collective-permute-start.21) | collective-permute-done | bytes 786464 | tf_op jit(solution)/shard_map/ppermute | solution.py:30
  84.3 5.3 %collective-permute-done.24 = f16[64,3072]{1,0:T(8,128)(2,1)S(1)} collective-permute-done((f16[64,3072]{1,0:T(8,128)(2,1)S(1)}, f16[64,3072]{1,0:T(8,128)(2,1)S(1)}, u32[]{:S(2)}, u32[]{:S(2)}) %collective-permute-start.24) | collective-permute-done | bytes 393248 | tf_op jit(solution)/shard_map/ppermute | solution.py:30
  95.4 3.5 %collective-permute-done.27 = bf16[32,3072]{1,0:T(8,128)(2,1)S(1)} collective-permute-done((bf16[32,3072]{1,0:T(8,128)(2,1)S(1)}, bf16[32,3072]{1,0:T(8,128)(2,1)S(1)}, u32[]{:S(2)}, u32[]{:S(2)}) %collective-permute-start.27) | collective-permute-done | bytes 196640 | tf_op jit(solution)/shard_map/ppermute | solution.py:30
  101.8 15.1 %collective-permute-done.34 = bf16[64,3072]{1,0:T(8,128)(2,1)S(1)} collective-permute-done((bf16[64,3072]{1,0:T(8,128)(2,1)S(1)}, bf16[64,3072]{1,0:T(8,128)(2,1)S(1)}, u32[]{:S(2)}, u32[]{:S(2)}) %collective-permute-start.34) | collective-permute-done | bytes 393248 | tf_op jit(solution)/shard_map/ppermute | solution.py:30
  126.2 2.8 %collective-permute-done.36 = bf16[128,3072]{1,0:T(8,128)(2,1)S(1)} collective-permute-done((bf16[128,3072]{1,0:T(8,128)(2,1)S(1)}, bf16[128,3072]{1,0:T(8,128)(2,1)S(1)}, u32[]{:S(2)}, u32[]{:S(2)}) %collective-permute-start.36) | collective-permute-done | bytes 786464 | tf_op jit(solution)/shard_map/ppermute | solution.py:30
  133.9 2.5 %collective-permute-start.41 = (bf16[128,3072]{1,0:T(8,128)(2,1)S(1)}, bf16[128,3072]{1,0:T(8,128)(2,1)S(1)}, u32[]{:S(2)}, u32[]{:S(2)}) collective-permute-start(bf16[128,3072]{1,0:T(8,128)(2,1)S(1)} %pad_maximum_fusion.15), channel_id=1, source_target_pairs={{0,16},{1,49},{16,0},{17,33},{32,48},{33,17},{48,32},{49,1},{64,80... | collective-permute-start | bytes 2359304 | tf_op jit(solution)/shard_map/ppermute | solution.py:30
  142.3 3.7 %collective-permute-done.41 = bf16[128,3072]{1,0:T(8,128)(2,1)S(1)} collective-permute-done((bf16[128,3072]{1,0:T(8,128)(2,1)S(1)}, bf16[128,3072]{1,0:T(8,128)(2,1)S(1)}, u32[]{:S(2)}, u32[]{:S(2)}) %collective-permute-start.41) | collective-permute-done | bytes 786464 | tf_op jit(solution)/shard_map/ppermute | solution.py:30
  150.5 2.4 %collective-permute-start.42 = (bf16[2,32,768]{2,1,0:T(8,128)(2,1)S(1)}, bf16[2,32,768]{2,1,0:T(8,128)(2,1)S(1)}, u32[]{:S(2)}, u32[]{:S(2)}) collective-permute-start(bf16[2,32,768]{2,1,0:T(8,128)(2,1)S(1)} %fusion.52), channel_id=1, source_target_pairs={{0,2},{1,3},{2,0},{3,1},{4,6},{5,7},{6,4},{7,5},{8,10},{9,11},{10,... | collective-permute-start | bytes 294920 | tf_op jit(solution)/shard_map/ppermute | solution.py:34
  154.6 7.0 %collective-permute-done.43 = bf16[2,128,768]{2,1,0:T(8,128)(2,1)S(1)} collective-permute-done((bf16[2,128,768]{2,1,0:T(8,128)(2,1)S(1)}, bf16[2,128,768]{2,1,0:T(8,128)(2,1)S(1)}, u32[]{:S(2)}, u32[]{:S(2)}) %collective-permute-start.43) | collective-permute-done | bytes 393248 | tf_op jit(solution)/shard_map/ppermute | solution.py:34
  168.4 3.1 %collective-permute-done.48 = bf16[2,32,768]{2,1,0:T(8,128)(2,1)S(1)} collective-permute-done((bf16[2,32,768]{2,1,0:T(8,128)(2,1)S(1)}, bf16[2,32,768]{2,1,0:T(8,128)(2,1)S(1)}, u32[]{:S(2)}, u32[]{:S(2)}) %collective-permute-start.48) | collective-permute-done | bytes 98336 | tf_op jit(solution)/shard_map/ppermute | solution.py:34
  171.7 8.5 %collective-permute-start.51 = (f32[128,768]{1,0:T(8,128)S(1)}, f32[128,768]{1,0:T(8,128)S(1)}, u32[]{:S(2)}, u32[]{:S(2)}) collective-permute-start(f32[128,768]{1,0:T(8,128)S(1)} %slice_bitcast_fusion), channel_id=1, source_target_pairs={{0,1},{1,0},{2,3},{3,2},{4,5},{5,4},{6,7},{7,6},{8,9},{9,8},{10,11... | collective-permute-start | bytes 1179656 | tf_op jit(solution)/shard_map/ppermute | solution.py:156
  (209 shorter events, 69.8 us)
Async XLA Ops:
  3.7 21.5 %collective-permute-start.6 = (bf16[768,3072]{1,0:T(8,128)(2,1)}, bf16[768,3072]{1,0:T(8,128)(2,1)}, u32[]{:S(2)}, u32[]{:S(2)}) collective-permute-start(bf16[768,3072]{1,0:T(8,128)(2,1)} %own.7), channel_id=1, source_target_pairs={{0,1},{1,0},{2,3},{3,2},{4,5},{5,4},{6,7},{7,6},{8,9},{9,8},{10,11... | collective-permute-start | bytes 14155784 | tf_op jit(solution)/shard_map/ppermute | solution.py:119
  17.5 19.3 %collective-permute-start.10 = (bf16[32,1536]{1,0:T(8,128)(2,1)S(1)}, bf16[32,1536]{1,0:T(8,128)(2,1)S(1)}, u32[]{:S(2)}, u32[]{:S(2)}) collective-permute-start(bf16[32,1536]{1,0:T(8,128)(2,1)S(1)} %get-tuple-element.391), channel_id=1, source_target_pairs={{0,2},{1,3},{2,0},{3,1},{4,6},{5,7},{6,4},{7,5},{8,10},{9,11},{10,... | collective-permute-start | bytes 294920 | tf_op jit(solution)/shard_map/ppermute | solution.py:34
  23.6 16.0 %collective-permute-start.12 = (bf16[128,1536]{1,0:T(8,128)(2,1)S(1)}, bf16[128,1536]{1,0:T(8,128)(2,1)S(1)}, u32[]{:S(2)}, u32[]{:S(2)}) collective-permute-start(bf16[128,1536]{1,0:T(8,128)(2,1)S(1)} %bitcast.308), channel_id=1, source_target_pairs={{0,12},{1,5},{2,14},{3,7},{4,8},{5,1},{6,10},{7,3},{8,4},{9,13},{1... | collective-permute-start | bytes 1179656 | tf_op jit(solution)/shard_map/ppermute | solution.py:34
  23.7 23.4 %collective-permute-start.14 = (bf16[128,1536]{1,0:T(8,128)(2,1)S(1)}, bf16[128,1536]{1,0:T(8,128)(2,1)S(1)}, u32[]{:S(2)}, u32[]{:S(2)}) collective-permute-start(bf16[128,1536]{1,0:T(8,128)(2,1)S(1)} %bitcast.304), channel_id=1, source_target_pairs={{0,12},{1,5},{2,14},{3,7},{4,8},{5,1},{6,10},{7,3},{8,4},{9,13},{1... | collective-permute-start | bytes 1179656 | tf_op jit(solution)/shard_map/ppermute | solution.py:34
  32.9 13.2 %collective-permute-start.9 = (f16[128,3072]{1,0:T(8,128)(2,1)S(1)}, f16[128,3072]{1,0:T(8,128)(2,1)S(1)}, u32[]{:S(2)}, u32[]{:S(2)}) collective-permute-start(f16[128,3072]{1,0:T(8,128)(2,1)S(1)} %convert_element_type.204), channel_id=1, source_target_pairs={{0,16},{1,49},{16,0},{17,33},{32,48},{33,17},{48,32},{49,1},{64,80... | collective-permute-start | bytes 2359304 | tf_op jit(solution)/shard_map/ppermute | solution.py:30
  45.2 12.1 %collective-permute-start.17 = (f16[128,3072]{1,0:T(8,128)(2,1)S(1)}, f16[128,3072]{1,0:T(8,128)(2,1)S(1)}, u32[]{:S(2)}, u32[]{:S(2)}) collective-permute-start(f16[128,3072]{1,0:T(8,128)(2,1)S(1)} %convert_element_type.205), channel_id=1, source_target_pairs={{0,16},{1,49},{16,0},{17,33},{32,48},{33,17},{48,32},{49,1},{64,80... | collective-permute-start | bytes 2359304 | tf_op jit(solution)/shard_map/ppermute | solution.py:30
  45.3 71.6 %collective-permute-start.33 = (bf16[3072,768]{1,0:T(8,128)(2,1)S(1)}, bf16[3072,768]{1,0:T(8,128)(2,1)S(1)}, u32[]{:S(2)}, u32[]{:S(2)}) collective-permute-start(bf16[3072,768]{1,0:T(8,128)(2,1)S(1)} %bitcast.337), channel_id=1, source_target_pairs={{0,1},{1,0},{2,3},{3,2},{4,5},{5,4},{6,7},{7,6},{8,9},{9,8},{10,11... | collective-permute-start | bytes 14155784 | tf_op jit(solution)/shard_map/ppermute | solution.py:119
  45.5 12.1 %collective-permute-start.16 = (bf16[128,1536]{1,0:T(8,128)(2,1)S(1)}, bf16[128,1536]{1,0:T(8,128)(2,1)S(1)}, u32[]{:S(2)}, u32[]{:S(2)}) collective-permute-start(bf16[128,1536]{1,0:T(8,128)(2,1)S(1)} %bitcast.306), channel_id=1, source_target_pairs={{0,12},{1,5},{2,14},{3,7},{4,8},{5,1},{6,10},{7,3},{8,4},{9,13},{1... | collective-permute-start | bytes 1179656 | tf_op jit(solution)/shard_map/ppermute | solution.py:34
  46.5 19.6 %collective-permute-start.13 = (f16[64,3072]{1,0:T(8,128)(2,1)S(1)}, f16[64,3072]{1,0:T(8,128)(2,1)S(1)}, u32[]{:S(2)}, u32[]{:S(2)}) collective-permute-start(f16[64,3072]{1,0:T(8,128)(2,1)S(1)} %get-tuple-element.414), channel_id=1, source_target_pairs={{0,64},{1,65},{16,80},{17,81},{32,96},{33,97},{48,112},{49,113},{6... | collective-permute-start | bytes 1179656 | tf_op jit(solution)/shard_map/ppermute | solution.py:30
  52.5 13.3 %collective-permute-start.15 = (f16[128,3072]{1,0:T(8,128)(2,1)S(1)}, f16[128,3072]{1,0:T(8,128)(2,1)S(1)}, u32[]{:S(2)}, u32[]{:S(2)}) collective-permute-start(f16[128,3072]{1,0:T(8,128)(2,1)S(1)} %convert_element_type.207), channel_id=1, source_target_pairs={{0,16},{1,49},{16,0},{17,33},{32,48},{33,17},{48,32},{49,1},{64,80... | collective-permute-start | bytes 2359304 | tf_op jit(solution)/shard_map/ppermute | solution.py:30
  63.1 15.1 %collective-permute-start.20 = (f16[64,3072]{1,0:T(8,128)(2,1)S(1)}, f16[64,3072]{1,0:T(8,128)(2,1)S(1)}, u32[]{:S(2)}, u32[]{:S(2)}) collective-permute-start(f16[64,3072]{1,0:T(8,128)(2,1)S(1)} %get-tuple-element.456), channel_id=1, source_target_pairs={{0,64},{1,65},{16,80},{17,81},{32,96},{33,97},{48,112},{49,113},{6... | collective-permute-start | bytes 1179656 | tf_op jit(solution)/shard_map/ppermute | solution.py:30
  63.7 14.2 %collective-permute-start.21 = (f16[128,3072]{1,0:T(8,128)(2,1)S(1)}, f16[128,3072]{1,0:T(8,128)(2,1)S(1)}, u32[]{:S(2)}, u32[]{:S(2)}) collective-permute-start(f16[128,3072]{1,0:T(8,128)(2,1)S(1)} %convert_element_type.209), channel_id=1, source_target_pairs={{0,16},{1,49},{16,0},{17,33},{32,48},{33,17},{48,32},{49,1},{64,80... | collective-permute-start | bytes 2359304 | tf_op jit(solution)/shard_map/ppermute | solution.py:30
  66.2 14.6 %collective-permute-start.18 = (f16[32,3072]{1,0:T(8,128)(2,1)S(1)}, f16[32,3072]{1,0:T(8,128)(2,1)S(1)}, u32[]{:S(2)}, u32[]{:S(2)}) collective-permute-start(f16[32,3072]{1,0:T(8,128)(2,1)S(1)} %get-tuple-element.452), channel_id=1, source_target_pairs={{0,48},{1,17},{16,32},{17,1},{32,16},{33,49},{48,0},{49,33},{64,11... | collective-permute-start | bytes 589832 | tf_op jit(solution)/shard_map/ppermute | solution.py:30
  66.5 14.1 %collective-permute-start.19 = (f16[64,3072]{1,0:T(8,128)(2,1)S(1)}, f16[64,3072]{1,0:T(8,128)(2,1)S(1)}, u32[]{:S(2)}, u32[]{:S(2)}) collective-permute-start(f16[64,3072]{1,0:T(8,128)(2,1)S(1)} %get-tuple-element.454), channel_id=1, source_target_pairs={{0,64},{1,65},{16,80},{17,81},{32,96},{33,97},{48,112},{49,113},{6... | collective-permute-start | bytes 1179656 | tf_op jit(solution)/shard_map/ppermute | solution.py:30
  94.4 23.0 %collective-permute-start.30 = (bf16[64,3072]{1,0:T(8,128)(2,1)S(1)}, bf16[64,3072]{1,0:T(8,128)(2,1)S(1)}, u32[]{:S(2)}, u32[]{:S(2)}) collective-permute-start(bf16[64,3072]{1,0:T(8,128)(2,1)S(1)} %pad_maximum_fusion.21), channel_id=1, source_target_pairs={{0,64},{1,65},{16,80},{17,81},{32,96},{33,97},{48,112},{49,113},{6... | collective-permute-start | bytes 1179656 | tf_op jit(solution)/shard_map/ppermute | solution.py:30
  98.9 17.9 %collective-permute-start.34 = (bf16[64,3072]{1,0:T(8,128)(2,1)S(1)}, bf16[64,3072]{1,0:T(8,128)(2,1)S(1)}, u32[]{:S(2)}, u32[]{:S(2)}) collective-permute-start(bf16[64,3072]{1,0:T(8,128)(2,1)S(1)} %pad_maximum_fusion.22), channel_id=1, source_target_pairs={{0,64},{1,65},{16,80},{17,81},{32,96},{33,97},{48,112},{49,113},{6... | collective-permute-start | bytes 1179656 | tf_op jit(solution)/shard_map/ppermute | solution.py:30
  100.0 17.4 %collective-permute-start.29 = (bf16[128,3072]{1,0:T(8,128)(2,1)S(1)}, bf16[128,3072]{1,0:T(8,128)(2,1)S(1)}, u32[]{:S(2)}, u32[]{:S(2)}) collective-permute-start(bf16[128,3072]{1,0:T(8,128)(2,1)S(1)} %pad_maximum_fusion.12), channel_id=1, source_target_pairs={{0,16},{1,49},{16,0},{17,33},{32,48},{33,17},{48,32},{49,1},{64,80... | collective-permute-start | bytes 2359304 | tf_op jit(solution)/shard_map/ppermute | solution.py:30
  100.3 17.0 %collective-permute-start.32 = (bf16[32,3072]{1,0:T(8,128)(2,1)S(1)}, bf16[32,3072]{1,0:T(8,128)(2,1)S(1)}, u32[]{:S(2)}, u32[]{:S(2)}) collective-permute-start(bf16[32,3072]{1,0:T(8,128)(2,1)S(1)} %fusion.37), channel_id=1, source_target_pairs={{0,48},{1,17},{16,32},{17,1},{32,16},{33,49},{48,0},{49,33},{64,11... | collective-permute-start | bytes 589832 | tf_op jit(solution)/shard_map/ppermute | solution.py:30
  116.9 12.1 %collective-permute-start.36 = (bf16[128,3072]{1,0:T(8,128)(2,1)S(1)}, bf16[128,3072]{1,0:T(8,128)(2,1)S(1)}, u32[]{:S(2)}, u32[]{:S(2)}) collective-permute-start(bf16[128,3072]{1,0:T(8,128)(2,1)S(1)} %pad_maximum_fusion.13), channel_id=1, source_target_pairs={{0,16},{1,49},{16,0},{17,33},{32,48},{33,17},{48,32},{49,1},{64,80... | collective-permute-start | bytes 2359304 | tf_op jit(solution)/shard_map/ppermute | solution.py:30
  122.5 14.9 %collective-permute-start.39 = (bf16[128,3072]{1,0:T(8,128)(2,1)S(1)}, bf16[128,3072]{1,0:T(8,128)(2,1)S(1)}, u32[]{:S(2)}, u32[]{:S(2)}) collective-permute-start(bf16[128,3072]{1,0:T(8,128)(2,1)S(1)} %pad_maximum_fusion.14), channel_id=1, source_target_pairs={{0,16},{1,49},{16,0},{17,33},{32,48},{33,17},{48,32},{49,1},{64,80... | collective-permute-start | bytes 2359304 | tf_op jit(solution)/shard_map/ppermute | solution.py:30
  132.4 18.0 %collective-permute-start.38 = (bf16[2,64,768]{2,1,0:T(8,128)(2,1)S(1)}, bf16[2,64,768]{2,1,0:T(8,128)(2,1)S(1)}, u32[]{:S(2)}, u32[]{:S(2)}) collective-permute-start(bf16[2,64,768]{2,1,0:T(8,128)(2,1)S(1)} %bitcast.332), channel_id=1, source_target_pairs={{0,12},{1,5},{2,14},{3,7},{4,8},{5,1},{6,10},{7,3},{8,4},{9,13},{1... | collective-permute-start | bytes 589832 | tf_op jit(solution)/shard_map/ppermute | solution.py:34
  133.9 12.1 %collective-permute-start.41 = (bf16[128,3072]{1,0:T(8,128)(2,1)S(1)}, bf16[128,3072]{1,0:T(8,128)(2,1)S(1)}, u32[]{:S(2)}, u32[]{:S(2)}) collective-permute-start(bf16[128,3072]{1,0:T(8,128)(2,1)S(1)} %pad_maximum_fusion.15), channel_id=1, source_target_pairs={{0,16},{1,49},{16,0},{17,33},{32,48},{33,17},{48,32},{49,1},{64,80... | collective-permute-start | bytes 2359304 | tf_op jit(solution)/shard_map/ppermute | solution.py:30
  136.4 16.5 %collective-permute-start.44 = (bf16[2,128,768]{2,1,0:T(8,128)(2,1)S(1)}, bf16[2,128,768]{2,1,0:T(8,128)(2,1)S(1)}, u32[]{:S(2)}, u32[]{:S(2)}) collective-permute-start(bf16[2,128,768]{2,1,0:T(8,128)(2,1)S(1)} %fusion.38), channel_id=1, source_target_pairs={{0,4},{1,13},{2,6},{3,15},{4,0},{5,9},{6,2},{7,11},{8,12},{9,5},{1... | collective-permute-start | bytes 1179656 | tf_op jit(solution)/shard_map/ppermute | solution.py:34
  150.5 21.1 %collective-permute-start.42 = (bf16[2,32,768]{2,1,0:T(8,128)(2,1)S(1)}, bf16[2,32,768]{2,1,0:T(8,128)(2,1)S(1)}, u32[]{:S(2)}, u32[]{:S(2)}) collective-permute-start(bf16[2,32,768]{2,1,0:T(8,128)(2,1)S(1)} %fusion.52), channel_id=1, source_target_pairs={{0,2},{1,3},{2,0},{3,1},{4,6},{5,7},{6,4},{7,5},{8,10},{9,11},{10,... | collective-permute-start | bytes 294920 | tf_op jit(solution)/shard_map/ppermute | solution.py:34
  (33 other events, 243.3 us)
